TPU v7x, 32 devices: a whole 2x2x4 slice. The times are simulated.
32 devices in a mesh: seq: 16 (over z, y, core), ch: 2 (over x).
Axes of the slice: x: 2, y: 2, z: 4, core: 2. Of those that a mesh axis runs over, the one named last changes fastest.
Arguments:
- inputs: bfloat16 [262144, 2048], P('seq', 'ch'), may hold values from -6 to 6
- first_factor: bfloat16 [512, 512], P('ch'), may hold values from -0.25 to 0.25
- twiddle: float32 [512, 512], P('seq'), may hold values from -4 to 4
- second_factor: bfloat16 [512, 512], P('ch'), may hold values from -0.25 to 0.25
- block_first: bfloat16 [64, 32, 32], P('ch'), may hold values from -1 to 1
- block_second: bfloat16 [32, 64, 64], P('ch'), may hold values from -0.75 to 0.75
Outputs:
- mixed_out: bfloat16 [262144, 2048], P('seq', 'ch')
All inputs are finite; a program needn't handle non-finite values.
Results may differ from a plain program's by a relative error of at most 0.007.
Values may be sent and summed in bfloat16 or wider, within the bound.
A program may use at most 576 MiB of HBM per device.

v0:
```python
import jax
import jax.numpy as jnp
from jax import lax
from jax.sharding import PartitionSpec as P

BLOCK = 512


def local(inputs, first_factor, twiddle, second_factor, block_first, block_second):
    tok_rows, channels = inputs.shape
    outer_rows = tok_rows // BLOCK
    token_grid = inputs.reshape(outer_rows, BLOCK, channels)
    contract = (((1,), (1,)), ((), ()))
    first = lax.dot_general(
        lax.all_gather(first_factor, "ch", axis=0, tiled=True),
        token_grid,
        contract,
        preferred_element_type=jnp.float32,
    )
    full_second = lax.all_gather(second_factor, "ch", axis=0, tiled=True)
    twisted = (first * jnp.transpose(twiddle)[:, :, None]).astype(jnp.bfloat16)
    mixed = lax.dot_general(
        full_second,
        lax.all_to_all(twisted, "seq", split_axis=0, concat_axis=1, tiled=True),
        contract,
        preferred_element_type=jnp.float32,
    )
    second = mixed.astype(jnp.bfloat16)
    returned = lax.all_to_all(second, "seq", split_axis=0, concat_axis=1, tiled=True)
    gated = (token_grid.astype(jnp.float32) * returned.astype(jnp.float32)).astype(jnp.bfloat16)
    grouped = gated.reshape(tok_rows, block_first.shape[0], block_first.shape[2])
    block_mix = jnp.einsum(
        "amb,tab->mat", block_first, grouped, preferred_element_type=jnp.float32
    ).astype(jnp.bfloat16)
    result_rows = jnp.einsum(
        "mpa,mat->tmp",
        block_second,
        lax.all_to_all(block_mix, "ch", split_axis=0, concat_axis=1, tiled=True),
        preferred_element_type=jnp.float32,
    )
    return result_rows.reshape(tok_rows, channels).astype(jnp.bfloat16)


def solution(mesh):
    placed = (
        P("seq", "ch"),
        P("ch", None),
        P("seq", None),
        P("ch", None),
        P("ch", None, None),
        P("ch", None, None),
    )
    return jax.shard_map(
        local, mesh=mesh, in_specs=placed, out_specs=P("seq", "ch"), check_vma=False
    )
```

profile of v0, /device:TPU:12, one launch (start us, length us, event | category | flops | bytes accessed | tf_op | source)
XLA Modules:
  0.0 2592.4 jit_solution(12671389983302678126)
XLA Ops:
  0.0 0.0 copy-start
  0.0 9.1 all_gather.6
  9.1 28.9 %multiply_convert_fusion = bf16[512,32,1024]{2,0,1:T(8,128)(2,1)} fusion(f32[512,32]{0,1:T(8,128)} %bitcast.46, bf16[32,512,1024]{2,1,0:T(8,128)(2,1)} %bitcast.44, bf16[512,512]{1,0:T(8,128)(2,1)S(1)} %all_gather.6), kind=kOutput, calls=%fused_computation.3 | convolution fusion | flops 17213423616 | bytes 67698688 | tf_op jit(solution)/shard_map/dot_general | solution.py:14
  38.0 30.8 %copy.30 = bf16[512,32,1024]{2,1,0:T(8,128)(2,1)} copy(bf16[512,32,1024]{2,0,1:T(8,128)(2,1)} %multiply_convert_fusion) | data formatting | bytes 67108864 | tf_op jit(solution)/shard_map/convert_element_type | solution.py:21
  68.8 0.0 copy-start.2
  68.8 6.4 all-to-all-start
  75.2 0.0 copy-done.2
  75.2 9.0 all_gather.7
  84.2 712.5 %all-to-all-done = bf16[512,32,1024]{2,1,0:T(8,128)(2,1)} async-done(((bf16[512,32,1024]{2,1,0:T(8,128)(2,1)}), bf16[512,32,1024]{2,1,0:T(8,128)(2,1)}, u32[]{:S(2)}, u32[]{:S(2)}) %all-to-all-start) | async-done | bytes 33554464 | tf_op jit(solution)/shard_map/all_to_all | solution.py:24
  796.7 22.8 copy.31
  819.5 28.9 %convert_bitcast_fusion.2 = bf16[512,32,1024]{0,2,1:T(8,128)(2,1)} fusion(bf16[32,512,1024]{2,1,0:T(8,128)(2,1)} %bitcast.45, bf16[512,512]{1,0:T(8,128)(2,1)S(1)} %all_gather.7), kind=kOutput, calls=%fused_computation.6 | convolution fusion | flops 17196646400 | bytes 67633152 | tf_op jit(solution)/shard_map/dot_general | solution.py:22
  848.3 46.4 %copy.33 = bf16[512,32,1024]{2,1,0:T(8,128)(2,1)} copy(bf16[512,32,1024]{0,2,1:T(8,128)(2,1)} %convert_bitcast_fusion.2) | data formatting | bytes 67108864 | tf_op jit(solution)/shard_map/convert_element_type | solution.py:28
  894.7 6.0 all-to-all-start.1
  900.7 44.1 %copy.29 = bf16[16384,1024]{0,1:T(8,128)(2,1)} copy(bf16[16384,1024]{1,0:T(8,128)(2,1)} %param.6) | data formatting | bytes 67108864 | tf_op args[0]
  944.8 677.2 %all-to-all-done.1 = bf16[512,32,1024]{2,1,0:T(8,128)(2,1)} async-done(((bf16[512,32,1024]{2,1,0:T(8,128)(2,1)}), bf16[512,32,1024]{2,1,0:T(8,128)(2,1)}, u32[]{:S(2)}, u32[]{:S(2)}) %all-to-all-start.1) | async-done | bytes 33554464 | tf_op jit(solution)/shard_map/all_to_all | solution.py:29
  1622.0 32.4 %convert_bitcast_fusion = f32[32,16,32,1024]{3,2,0,1:T(8,128)} fusion(bf16[16,32,32,1024]{3,2,1,0:T(8,128)(2,1)} %bitcast.19), kind=kLoop, calls=%fused_computation | loop fusion | flops 16777216 | bytes 100663296 | tf_op jit(solution)/shard_map/convert_element_type | solution.py:30
  1654.5 195.2 %copy.40 = f32[32,16,32,1024]{2,1,0,3:T(8,128)} copy(f32[32,16,32,1024]{3,2,0,1:T(8,128)} %convert_bitcast_fusion) | data formatting | bytes 134217728 | tf_op jit(solution)/shard_map/convert_element_type | solution.py:30
  1849.6 184.7 %reshape.21 = f32[16384,32,32]{0,2,1:T(8,128)} reshape(f32[32,16,32,1024]{2,1,0,3:T(8,128)} %copy.40) | data formatting | bytes 134217728 | tf_op jit(solution)/shard_map/convert_element_type | solution.py:30
  2034.3 0.0 copy-done
  2034.3 44.1 %convert_bitcast_fusion.1 = bf16[32,32,16384]{2,0,1:T(8,128)(2,1)} fusion(bf16[32,32,32]{2,1,0:T(8,128)(2,1)S(1)} %copy-done, f32[16384,32,32]{0,2,1:T(8,128)} %reshape.21, bf16[16384,32,32]{0,2,1:T(8,128)(2,1)} %bitcast.40), kind=kOutput, calls=%fused_computation.5 | convolution fusion | flops 1140850688 | bytes 134283264 | tf_op jit(solution)/shard_map/amb,tab->mat/dot_general | solution.py:32
  2078.4 29.3 %copy.36 = bf16[32,32,16384]{2,1,0:T(8,128)(2,1)} copy(bf16[32,32,16384]{2,0,1:T(8,128)(2,1)} %convert_bitcast_fusion.1) | data formatting | bytes 67108864 | tf_op jit(solution)/shard_map/convert_element_type | solution.py:34
  2107.7 394.9 %all_to_all.45 = bf16[32,32,16384]{2,1,0:T(8,128)(2,1)} all-to-all(bf16[32,32,16384]{2,1,0:T(8,128)(2,1)} %copy.36), channel_id=1, replica_groups=mesh['seq'=16,'ch'=2] {'ch'}, dimensions={0} | all-to-all | bytes 67108864 | tf_op jit(solution)/shard_map/all_to_all | solution.py:38
  2502.7 0.0 copy-start.1
  2502.7 22.9 copy.37
  2525.6 0.0 copy-done.1
  2525.6 22.9 convolution_convert_fusion
  2548.5 43.9 %copy.38 = bf16[16384,1024]{1,0:T(8,128)(2,1)} copy(bf16[16384,1024]{0,1:T(8,128)(2,1)} %bitcast.43) | data formatting | bytes 67108864 | tf_op jit(solution)/shard_map/convert_element_type | solution.py:41
Async XLA Ops:
  0.0 2034.3 %copy-start = (bf16[32,32,32]{2,1,0:T(8,128)(2,1)S(1)}, bf16[32,32,32]{2,1,0:T(8,128)(2,1)}, u32[]{:S(2)}) copy-start(bf16[32,32,32]{2,1,0:T(8,128)(2,1)} %param.10) | copy-start | bytes 196612
  68.8 6.4 copy-start.2
  68.8 727.9 %all-to-all-start = ((bf16[512,32,1024]{2,1,0:T(8,128)(2,1)}), bf16[512,32,1024]{2,1,0:T(8,128)(2,1)}, u32[]{:S(2)}, u32[]{:S(2)}) async-start(bf16[512,32,1024]{2,1,0:T(8,128)(2,1)} %copy.30), calls=%async_computation | async-start | bytes 67108864 | tf_op jit(solution)/shard_map/all_to_all | solution.py:24
  894.7 727.3 %all-to-all-start.1 = ((bf16[512,32,1024]{2,1,0:T(8,128)(2,1)}), bf16[512,32,1024]{2,1,0:T(8,128)(2,1)}, u32[]{:S(2)}, u32[]{:S(2)}) async-start(bf16[512,32,1024]{2,1,0:T(8,128)(2,1)} %copy.33), calls=%async_computation.1 | async-start | bytes 67108864 | tf_op jit(solution)/shard_map/all_to_all | solution.py:29
  2502.7 22.9 copy-start.1
where the time goes:
time: 2600 us; the launch traced here: 2590 us
  waiting for transfers between devices  1390 us (53%)
  local copies, waits for them, and re-layouts  620 us (24%)
  blocking collectives  413 us (16%)
  matrix products  125 us (5%)
  other arithmetic  32.4 us (1%)
    all_to_all x1, waiting for transfers between devices, local(): lax.all_to_all(twisted, 'seq', split_axis=0, concat_axis=1, tiled=True)  712 us
    all_to_all x1, waiting for transfers between devices, local(): lax.all_to_all(second, 'seq', split_axis=0, concat_axis=1, tiled=True)  677 us
    all_to_all x1, blocking collectives, local(): lax.all_to_all(block_mix, 'ch', split_axis=0, concat_axis=1, tiled=True)  395 us
    convert_element_type x2, local copies, waits for them, and re-layouts, local(): returned.astype(jnp.float32)  380 us
  transfers between devices with their start and end apart: 2, of which 2 were waited for; matrix products, arithmetic and copies ran while one was open for 2% of the time, Pallas kernels for 0%

commit v1 on v0

v1 whole, which is shorter than its diff:
```python
import jax
import jax.numpy as jnp
from jax import lax
from jax.sharding import PartitionSpec as P

BLOCK = 512
CHUNKS = 4


def local(inputs, first_factor, twiddle, second_factor, block_first, block_second):
    tok_rows, channels = inputs.shape
    outer_rows = tok_rows // BLOCK
    n_ch = lax.axis_size("ch")
    me = lax.axis_index("ch")
    a_loc, m_all, b_all = block_first.shape
    m_loc, p_all, a_all = block_second.shape
    token_grid = inputs.reshape(outer_rows, BLOCK, channels)
    contract = (((1,), (1,)), ((), ()))
    full_first = lax.all_gather(first_factor, "ch", axis=0, tiled=True)
    full_second = lax.all_gather(second_factor, "ch", axis=0, tiled=True)
    twiddle_t = jnp.transpose(twiddle)
    k_sub = BLOCK // CHUNKS

    eye_a = jnp.eye(a_loc, dtype=jnp.bfloat16)
    eye_m = jnp.eye(m_loc, dtype=jnp.bfloat16)
    first_dense, second_dense = [], []
    for shift in range(n_ch):
        to = lax.rem(me + shift, n_ch)
        source = lax.rem(me + n_ch - shift, n_ch)
        piece = lax.dynamic_slice_in_dim(block_first, to * m_loc, m_loc, 1)
        piece = jnp.transpose(piece, (0, 2, 1))[:, :, :, None] * eye_a[:, None, None, :]
        first_dense.append(piece.reshape(a_loc * b_all, m_loc * a_loc))
        piece = lax.dynamic_slice_in_dim(block_second, source * a_loc, a_loc, 2)
        piece = jnp.transpose(piece, (0, 2, 1))[:, :, None, :] * eye_m[:, None, :, None]
        second_dense.append(piece.reshape(m_loc * a_loc, m_loc * p_all))

    sent = []
    for q in range(CHUNKS):
        ks = slice(q * k_sub, (q + 1) * k_sub)
        first = lax.dot_general(
            full_first[ks], token_grid, contract, preferred_element_type=jnp.float32
        )
        twisted = (first * twiddle_t[ks][:, :, None]).astype(jnp.bfloat16)
        if q >= 2:
            twisted, sent[q - 2] = lax.optimization_barrier((twisted, sent[q - 2]))
        sent.append(lax.all_to_all(twisted, "seq", split_axis=0, concat_axis=1, tiled=True))

    by_owner = full_second.reshape(BLOCK // outer_rows, outer_rows, BLOCK)
    half = outer_rows // 2
    steps = [(q, 0, outer_rows) for q in range(CHUNKS - 1)]
    steps += [(CHUNKS - 1, 0, half), (CHUNKS - 1, half, outer_rows - half)]
    results, received = [], []
    for n, (q, low, rows) in enumerate(steps):
        ks = slice(q * k_sub, (q + 1) * k_sub)
        factor = by_owner[:, low : low + rows].reshape(-1, BLOCK)
        second = lax.dot_general(
            factor, sent[q], contract, preferred_element_type=jnp.float32
        ).astype(jnp.bfloat16)
        if n >= 2:
            second, received[n - 2] = lax.optimization_barrier((second, received[n - 2]))
        returned = lax.all_to_all(second, "seq", split_axis=0, concat_axis=1, tiled=True)
        gated = (
            token_grid[low : low + rows, ks].astype(jnp.float32)
            * returned.astype(jnp.float32)
        ).astype(jnp.bfloat16)
        gated = gated.reshape(rows * k_sub, channels)
        parts = []
        for shift in range(n_ch):
            middle = jnp.dot(
                gated, first_dense[shift], preferred_element_type=jnp.float32
            ).astype(jnp.bfloat16)
            if shift:
                middle = lax.ppermute(
                    middle, "ch", [(d, (d + shift) % n_ch) for d in range(n_ch)]
                )
            parts.append(middle)
        received.append(parts)
    for n, (q, low, rows) in enumerate(steps):
        total = None
        for shift in range(n_ch):
            term = jnp.dot(
                received[n][shift], second_dense[shift], preferred_element_type=jnp.float32
            )
            total = term if total is None else total + term
        results.append(total.astype(jnp.bfloat16).reshape(rows, k_sub, channels))
    results[-2:] = [jnp.concatenate(results[-2:], axis=0)]
    return jnp.concatenate(results, axis=1).reshape(tok_rows, channels)


def solution(mesh):
    placed = (
        P("seq", "ch"),
        P("ch", None),
        P("seq", None),
        P("ch", None),
        P("ch", None, None),
        P("ch", None, None),
    )
    return jax.shard_map(
        local, mesh=mesh, in_specs=placed, out_specs=P("seq", "ch"), check_vma=False
    )
```

time: 2600 us -> 1750 us (0.67)
  local copies, waits for them, and re-layouts: 620 us -> 153 us
  blocking collectives: 413 us -> 18 us
  waiting for transfers between devices: 1390 us -> 1170 us
  matrix products: 125 us -> 263 us
  other arithmetic: 32.4 us -> 76.9 us
  starting transfers between devices: 12.4 us -> 56.7 us
    convert_element_type x6 -> x4, local copies, waits for them, and re-layouts: 530 us -> 47.9 us  [the longest x2 25.1 us: local(): second = lax.dot_general(factor, sent[q], contract, preferred_element_typ...]
    all_to_all x1 -> x0, blocking collectives: 395 us -> none  [local(): lax.all_to_all(block_mix, 'ch', split_axis=0, concat_axis=1, tiled=True)]
    all_to_all x1 -> x5, waiting for transfers between devices: 677 us -> 387 us  [local(): lax.all_to_all(second, 'seq', split_axis=0, concat_axis=1, tiled=True)]
    ppermute x0 -> x5, waiting for transfers between devices: none -> 178 us  [local(): lax.ppermute(middle, 'ch', [(d, (d + shift) % n_ch) for d in range(n_ch)])]
    dot_general x4 -> x27, matrix products: 125 us -> 263 us  [the longest x10 103 us: local(): jnp.dot(received[n][shift], second_dense[shift], preferred_element_type=j...]
    all_to_all x1 -> x4, waiting for transfers between devices: 712 us -> 607 us  [local(): lax.all_to_all(twisted, 'seq', split_axis=0, concat_axis=1, tiled=True)]
    optimization_barrier x0 -> x5, local copies, waits for them, and re-layouts: none -> 49.3 us  [the longest x3 26.6 us: local(): lax.optimization_barrier((second, received[n - 2]))]
    unnamed x7 -> x40, local copies, waits for them, and re-layouts: 44.1 us -> 0.08 us
  transfers between devices with their start and end apart: 2 -> 14, of which waited for: 2 -> 12; matrix products, arithmetic and copies ran while one was open for 2% -> 23% of each run, Pallas kernels for 0% -> 0%
where the time goes in v1:
time: 1750 us; the launch traced here: 1740 us
  waiting for transfers between devices  1170 us (67%)
  matrix products  263 us (15%)
  local copies, waits for them, and re-layouts  153 us (9%)
  other arithmetic  76.9 us (4%)
  starting transfers between devices  56.7 us (3%)
  blocking collectives  18 us (1%)
    all_to_all x4, waiting for transfers between devices, local(): lax.all_to_all(twisted, 'seq', split_axis=0, concat_axis=1, tiled=True)  607 us
    all_to_all x5, waiting for transfers between devices, local(): lax.all_to_all(second, 'seq', split_axis=0, concat_axis=1, tiled=True)  387 us
    ppermute x5, waiting for transfers between devices, local(): lax.ppermute(middle, 'ch', [(d, (d + shift) % n_ch) for d in range(n_ch)])  178 us
    dot_general x10, matrix products, local(): jnp.dot(received[n][shift], second_dense[shift], preferred_element_type=j...  103 us
    dot_general x4, matrix products, local(): lax.dot_general(full_first[ks], token_grid, contract, preferred_element_t...  65.8 us
    dot_general x8, matrix products, local(): jnp.dot(gated, first_dense[shift], preferred_element_type=jnp.float32)  47.8 us
    dot_general x5, matrix products, local(): lax.dot_general(factor, sent[q], contract, preferred_element_type=jnp.flo...  46.7 us
    concatenate x1, other arithmetic, local(): return jnp.concatenate(results, axis=1).reshape(tok_rows, channels)  35.3 us
  transfers between devices with their start and end apart: 14, of which 12 were waited for; matrix products, arithmetic and copies ran while one was open for 23% of the time, Pallas kernels for 0%

profile of v1, /device:TPU:12, one launch (start us, length us, event | category | flops | bytes accessed | tf_op | source)
XLA Modules:
  0.0 1741.4 jit_solution(136023543443068535)
XLA Ops:
  0.8 8.9 all_gather.6
  9.7 16.4 multiply_convert_fusion.2
  26.1 11.4 copy.84
  37.5 6.6 all-to-all-start
  44.1 16.4 multiply_convert_fusion
  60.6 11.4 copy.96
  72.0 154.2 %all-to-all-done = bf16[128,32,1024]{2,1,0:T(8,128)(2,1)} async-done(((bf16[128,32,1024]{2,1,0:T(8,128)(2,1)}), bf16[128,32,1024]{2,1,0:T(8,128)(2,1)}, u32[]{:S(2)}, u32[]{:S(2)}) %all-to-all-start) | async-done | bytes 8388640 | tf_op jit(solution)/shard_map/all_to_all | solution.py:46
  226.2 5.4 all-to-all-start.3
  231.6 16.4 multiply_convert_fusion.3
  248.0 8.5 copy.85
  256.6 11.4 copy.86
  268.0 145.7 %all-to-all-done.3 = bf16[128,32,1024]{2,1,0:T(8,128)(2,1)} async-done(((bf16[128,32,1024]{2,1,0:T(8,128)(2,1)}), bf16[128,32,1024]{2,1,0:T(8,128)(2,1)}, u32[]{:S(2)}, u32[]{:S(2)}) %all-to-all-start.3) | async-done | bytes 8388640 | tf_op jit(solution)/shard_map/all_to_all | solution.py:46
  418.7 9.0 all_gather.7
  427.7 10.2 convert_bitcast_fusion.6
  438.0 12.6 copy.90
  450.5 150.4 %all-to-all-done.1 = bf16[128,32,1024]{2,1,0:T(8,128)(2,1)} async-done(((bf16[128,32,1024]{2,1,0:T(8,128)(2,1)}), bf16[128,32,1024]{2,1,0:T(8,128)(2,1)}, u32[]{:S(2)}, u32[]{:S(2)}) %all-to-all-start.1) | async-done | bytes 8388640 | tf_op jit(solution)/shard_map/all_to_all | solution.py:46
  600.9 5.7 all-to-all-start.2
  606.6 16.4 multiply_convert_fusion.1
  623.0 8.6 copy.97
  631.6 10.2 convert_bitcast_fusion.5
  641.8 12.6 copy.102
  654.4 134.2 %all-to-all-done.2 = bf16[512,8,1024]{2,1,0:T(8,128)(2,1)} async-done(((bf16[512,8,1024]{2,1,0:T(8,128)(2,1)}), bf16[512,8,1024]{2,1,0:T(8,128)(2,1)}, u32[]{:S(2)}, u32[]{:S(2)}) %all-to-all-start.2) | async-done | bytes 8388640 | tf_op jit(solution)/shard_map/all_to_all | solution.py:61
  794.4 7.0 broadcast_multiply_fusion
  801.4 5.9 mul.184
  807.3 7.9 fusion.2
  815.2 6.1 convolution_convert_fusion.4
  822.8 6.8 mul.180
  829.6 8.7 copy.87
  838.3 10.4 convert_bitcast_fusion.7
  848.7 6.3 convolution_convert_fusion.5
  855.1 59.2 %collective-permute-done = bf16[4096,512]{1,0:T(8,128)(2,1)} collective-permute-done((bf16[4096,512]{1,0:T(8,128)(2,1)}, bf16[4096,512]{1,0:T(8,128)(2,1)}, u32[]{:S(2)}, u32[]{:S(2)}) %collective-permute-start) | collective-permute-done | bytes 4194336 | tf_op jit(solution)/shard_map/ppermute | solution.py:73
  914.3 12.5 copy.105
  926.8 49.2 %all-to-all-done.5 = bf16[512,8,1024]{2,1,0:T(8,128)(2,1)} async-done(((bf16[512,8,1024]{2,1,0:T(8,128)(2,1)}), bf16[512,8,1024]{2,1,0:T(8,128)(2,1)}, u32[]{:S(2)}, u32[]{:S(2)}) %all-to-all-start.5) | async-done | bytes 8388640 | tf_op jit(solution)/shard_map/all_to_all | solution.py:61
  981.1 11.4 copy.98
  992.5 170.8 %all-to-all-done.6 = bf16[512,8,1024]{2,1,0:T(8,128)(2,1)} async-done(((bf16[512,8,1024]{2,1,0:T(8,128)(2,1)}), bf16[512,8,1024]{2,1,0:T(8,128)(2,1)}, u32[]{:S(2)}, u32[]{:S(2)}) %all-to-all-start.6) | async-done | bytes 8388640 | tf_op jit(solution)/shard_map/all_to_all | solution.py:61
  1163.3 5.6 all-to-all-start.4
  1168.9 16.7 fusion.1
  1185.6 6.1 convolution_convert_fusion.2
  1193.9 157.0 %all-to-all-done.4 = bf16[128,32,1024]{2,1,0:T(8,128)(2,1)} async-done(((bf16[128,32,1024]{2,1,0:T(8,128)(2,1)}), bf16[128,32,1024]{2,1,0:T(8,128)(2,1)}, u32[]{:S(2)}, u32[]{:S(2)}) %all-to-all-start.4) | async-done | bytes 8388640 | tf_op jit(solution)/shard_map/all_to_all | solution.py:46
  1350.9 8.8 copy.99
  1359.7 7.9 convert_bitcast_fusion.9
  1367.7 6.1 convolution_convert_fusion.3
  1373.8 6.8 copy.107
  1386.6 9.4 convolution_convert_fusion
  1405.7 7.9 convert_bitcast_fusion.8
  1413.6 10.9 fusion.14
  1424.5 6.1 convolution_convert_fusion.1
  1430.6 58.4 %collective-permute-done.2 = bf16[4096,512]{1,0:T(8,128)(2,1)} collective-permute-done((bf16[4096,512]{1,0:T(8,128)(2,1)}, bf16[4096,512]{1,0:T(8,128)(2,1)}, u32[]{:S(2)}, u32[]{:S(2)}) %collective-permute-start.2) | collective-permute-done | bytes 4194336 | tf_op jit(solution)/shard_map/ppermute | solution.py:73
  1488.9 7.2 copy.109
  1496.1 6.0 all-to-all-start.8
  1502.1 15.2 add_convert_fusion.2
  1517.3 10.7 fusion.16
  1528.0 10.4 fusion.15
  1538.4 11.4 add_convert_fusion
  1549.9 11.4 add_convert_fusion.1
  1561.3 33.2 %all-to-all-done.8 = bf16[256,8,1024]{2,1,0:T(8,128)(2,1)} async-done(((bf16[256,8,1024]{2,1,0:T(8,128)(2,1)}), bf16[256,8,1024]{2,1,0:T(8,128)(2,1)}, u32[]{:S(2)}, u32[]{:S(2)}) %all-to-all-start.8) | async-done | bytes 4194336 | tf_op jit(solution)/shard_map/all_to_all | solution.py:61
  1594.5 8.2 fusion.4
  1612.3 10.3 fusion.5
  1622.7 10.1 fusion.6
  1632.8 22.7 %collective-permute-done.3 = bf16[2048,512]{1,0:T(8,128)(2,1)} collective-permute-done((bf16[2048,512]{1,0:T(8,128)(2,1)}, bf16[2048,512]{1,0:T(8,128)(2,1)}, u32[]{:S(2)}, u32[]{:S(2)}) %collective-permute-start.3) | collective-permute-done | bytes 2097184 | tf_op jit(solution)/shard_map/ppermute | solution.py:73
  1655.4 6.6 add_convert_fusion.4
  1662.0 37.7 %collective-permute-done.4 = bf16[2048,512]{1,0:T(8,128)(2,1)} collective-permute-done((bf16[2048,512]{1,0:T(8,128)(2,1)}, bf16[2048,512]{1,0:T(8,128)(2,1)}, u32[]{:S(2)}, u32[]{:S(2)}) %collective-permute-start.4) | collective-permute-done | bytes 2097184 | tf_op jit(solution)/shard_map/ppermute | solution.py:73
  1699.7 6.1 add_convert_fusion.3
  1705.8 35.3 %maximum_maximum_fusion = bf16[32,512,1024]{2,1,0:T(8,128)(2,1)} fusion(bf16[16,128,1024]{2,1,0:T(8,128)(2,1)} %bitcast.203, bf16[16,128,1024]{2,1,0:T(8,128)(2,1)S(1)} %bitcast.202, bf16[32,128,1024]{2,1,0:T(8,128)(2,1)} %bitcast.200, bf16[32,128,1024]{2,1,0:T(8,128)(2,1)} %bitcast.201, bf16[32,128,1024]{2,1,0:T(8,128)(2,1)} %bitcast.199), kind=kLoop, calls=%fused_computation | loop fusion | flops 167772160 | bytes 67108864 | tf_op jit(solution)/shard_map/concatenate | solution.py:87
  (69 shorter events, 45.6 us)
Async XLA Ops:
  37.5 188.7 %all-to-all-start = ((bf16[128,32,1024]{2,1,0:T(8,128)(2,1)}), bf16[128,32,1024]{2,1,0:T(8,128)(2,1)}, u32[]{:S(2)}, u32[]{:S(2)}) async-start(bf16[128,32,1024]{2,1,0:T(8,128)(2,1)} %copy.84), calls=%async_computation | async-start | bytes 16777216 | tf_op jit(solution)/shard_map/all_to_all | solution.py:46
  226.2 187.5 %all-to-all-start.3 = ((bf16[128,32,1024]{2,1,0:T(8,128)(2,1)}), bf16[128,32,1024]{2,1,0:T(8,128)(2,1)}, u32[]{:S(2)}, u32[]{:S(2)}) async-start(bf16[128,32,1024]{2,1,0:T(8,128)(2,1)} %copy.96), calls=%async_computation.3 | async-start | bytes 16777216 | tf_op jit(solution)/shard_map/all_to_all | solution.py:46
  268.0 150.7 %copy-start.11 = (bf16[256,512]{1,0:T(8,128)(2,1)S(1)}, bf16[256,512]{1,0:T(8,128)(2,1)}, u32[]{:S(2)}) copy-start(bf16[256,512]{1,0:T(8,128)(2,1)} %param.9) | copy-start | bytes 786436
  413.7 187.2 %all-to-all-start.1 = ((bf16[128,32,1024]{2,1,0:T(8,128)(2,1)}), bf16[128,32,1024]{2,1,0:T(8,128)(2,1)}, u32[]{:S(2)}, u32[]{:S(2)}) async-start(bf16[128,32,1024]{2,1,0:T(8,128)(2,1)} %copy.86), calls=%async_computation.1 | async-start | bytes 16777216 | tf_op jit(solution)/shard_map/all_to_all | solution.py:46
  600.9 187.7 %all-to-all-start.2 = ((bf16[512,8,1024]{2,1,0:T(8,128)(2,1)}), bf16[512,8,1024]{2,1,0:T(8,128)(2,1)}, u32[]{:S(2)}, u32[]{:S(2)}) async-start(bf16[512,8,1024]{2,1,0:T(8,128)(2,1)} %copy.90), calls=%async_computation.2 | async-start | bytes 16777216 | tf_op jit(solution)/shard_map/all_to_all | solution.py:61
  654.4 139.6 %copy-start.12 = (bf16[32,32,32]{2,1,0:T(8,128)(2,1)S(1)}, bf16[32,32,32]{2,1,0:T(8,128)(2,1)}, u32[]{:S(2)}) copy-start(bf16[32,32,32]{2,1,0:T(8,128)(2,1)} %param.10) | copy-start | bytes 196612
  788.6 187.4 %all-to-all-start.5 = ((bf16[512,8,1024]{2,1,0:T(8,128)(2,1)}), bf16[512,8,1024]{2,1,0:T(8,128)(2,1)}, u32[]{:S(2)}, u32[]{:S(2)}) async-start(bf16[512,8,1024]{2,1,0:T(8,128)(2,1)} %copy.102), calls=%async_computation.5 | async-start | bytes 16777216 | tf_op jit(solution)/shard_map/all_to_all | solution.py:61
  815.2 6.1 copy-start
  821.3 92.9 %collective-permute-start = (bf16[4096,512]{1,0:T(8,128)(2,1)}, bf16[4096,512]{1,0:T(8,128)(2,1)}, u32[]{:S(2)}, u32[]{:S(2)}) collective-permute-start(bf16[4096,512]{1,0:T(8,128)(2,1)} %convolution_convert_fusion.4), channel_id=1, source_target_pairs={{0,1},{1,0},{2,3},{3,2},{4,5},{5,4},{6,7},{7,6},{8,9},{9,8},{10,11... | collective-permute-start | bytes 12582920 | tf_op jit(solution)/shard_map/ppermute | solution.py:73
  829.6 19.1 %slice-start = ((s8[8388608]{0:T(1024)(128)(4,1)}), s8[4194304]{0:T(1024)(128)(4,1)S(1)}, s32[]{:S(2)}) async-start(s8[8388608]{0:T(1024)(128)(4,1)} %bitcast.183), calls=%async_computation.9 | async-start | bytes 8388608
  838.3 10.4 slice-start.1
  838.3 10.4 copy-start.4
  976.0 187.2 %all-to-all-start.6 = ((bf16[512,8,1024]{2,1,0:T(8,128)(2,1)}), bf16[512,8,1024]{2,1,0:T(8,128)(2,1)}, u32[]{:S(2)}, u32[]{:S(2)}) async-start(bf16[512,8,1024]{2,1,0:T(8,128)(2,1)} %copy.105), calls=%async_computation.6 | async-start | bytes 16777216 | tf_op jit(solution)/shard_map/all_to_all | solution.py:61
  1163.3 187.7 %all-to-all-start.4 = ((bf16[128,32,1024]{2,1,0:T(8,128)(2,1)}), bf16[128,32,1024]{2,1,0:T(8,128)(2,1)}, u32[]{:S(2)}, u32[]{:S(2)}) async-start(bf16[128,32,1024]{2,1,0:T(8,128)(2,1)} %copy.98), calls=%async_computation.4 | async-start | bytes 16777216 | tf_op jit(solution)/shard_map/all_to_all | solution.py:46
  1185.6 6.1 copy-start.1
  1191.7 182.1 %collective-permute-start.1 = (bf16[4096,512]{1,0:T(8,128)(2,1)}, bf16[4096,512]{1,0:T(8,128)(2,1)}, u32[]{:S(2)}, u32[]{:S(2)}) collective-permute-start(bf16[4096,512]{1,0:T(8,128)(2,1)} %convolution_convert_fusion.2), channel_id=1, source_target_pairs={{0,1},{1,0},{2,3},{3,2},{4,5},{5,4},{6,7},{7,6},{8,9},{9,8},{10,11... | collective-permute-start | bytes 12582920 | tf_op jit(solution)/shard_map/ppermute | solution.py:73
  1350.9 16.7 slice-start.4
  1359.7 7.9 slice-start.5
  1359.7 7.9 copy-start.5
  1373.8 12.2 copy-start.10
  1380.6 115.5 %all-to-all-start.7 = ((bf16[256,8,1024]{2,1,0:T(8,128)(2,1)}), bf16[256,8,1024]{2,1,0:T(8,128)(2,1)}, u32[]{:S(2)}, u32[]{:S(2)}) async-start(bf16[256,8,1024]{2,1,0:T(8,128)(2,1)} %copy.107), calls=%async_computation.7 | async-start | bytes 8388608 | tf_op jit(solution)/shard_map/all_to_all | solution.py:61
  1396.0 92.9 %collective-permute-start.2 = (bf16[4096,512]{1,0:T(8,128)(2,1)}, bf16[4096,512]{1,0:T(8,128)(2,1)}, u32[]{:S(2)}, u32[]{:S(2)}) collective-permute-start(bf16[4096,512]{1,0:T(8,128)(2,1)} %convolution_convert_fusion), channel_id=1, source_target_pairs={{0,1},{1,0},{2,3},{3,2},{4,5},{5,4},{6,7},{7,6},{8,9},{9,8},{10,11... | collective-permute-start | bytes 12582920 | tf_op jit(solution)/shard_map/ppermute | solution.py:73
  1405.7 8.0 copy-start.7
  1405.7 18.8 %slice-start.2 = ((s8[8388608]{0:T(1024)(128)(4,1)}), s8[4194304]{0:T(1024)(128)(4,1)S(1)}, s32[]{:S(2)}) async-start(s8[8388608]{0:T(1024)(128)(4,1)} %bitcast.192), calls=%async_computation.11 | async-start | bytes 8388608
  1413.6 10.9 slice-start.3
  1413.6 10.9 copy-start.6
  1496.1 98.3 %all-to-all-start.8 = ((bf16[256,8,1024]{2,1,0:T(8,128)(2,1)}), bf16[256,8,1024]{2,1,0:T(8,128)(2,1)}, u32[]{:S(2)}, u32[]{:S(2)}) async-start(bf16[256,8,1024]{2,1,0:T(8,128)(2,1)} %copy.109), calls=%async_computation.8 | async-start | bytes 8388608 | tf_op jit(solution)/shard_map/all_to_all | solution.py:61
  1528.0 10.4 copy-start.8
  1602.6 9.1 copy-start.2
  1602.7 9.1 copy-start.3
  1606.7 48.8 %collective-permute-start.3 = (bf16[2048,512]{1,0:T(8,128)(2,1)}, bf16[2048,512]{1,0:T(8,128)(2,1)}, u32[]{:S(2)}, u32[]{:S(2)}) collective-permute-start(bf16[2048,512]{1,0:T(8,128)(2,1)} %convolution_convert_fusion.8), channel_id=1, source_target_pairs={{0,1},{1,0},{2,3},{3,2},{4,5},{5,4},{6,7},{7,6},{8,9},{9,8},{10,11... | collective-permute-start | bytes 6291464 | tf_op jit(solution)/shard_map/ppermute | solution.py:73
  1611.8 10.9 copy-start.9
  1611.8 87.9 %collective-permute-start.4 = (bf16[2048,512]{1,0:T(8,128)(2,1)}, bf16[2048,512]{1,0:T(8,128)(2,1)}, u32[]{:S(2)}, u32[]{:S(2)}) collective-permute-start(bf16[2048,512]{1,0:T(8,128)(2,1)} %convolution_convert_fusion.6), channel_id=1, source_target_pairs={{0,1},{1,0},{2,3},{3,2},{4,5},{5,4},{6,7},{7,6},{8,9},{9,8},{10,11... | collective-permute-start | bytes 6291464 | tf_op jit(solution)/shard_map/ppermute | solution.py:73
  1632.8 67.0 %copy-start.13 = (f32[2048,1024]{1,0:T(8,128)S(1)}, f32[2048,1024]{1,0:T(8,128)}, u32[]{:S(2)}) copy-start(f32[2048,1024]{1,0:T(8,128)} %fusion.6) | copy-start | bytes 25165828

commit v2 on v1

--- a/solution.py
+++ b/solution.py
@@ -46,19 +46,41 @@
         sent.append(lax.all_to_all(twisted, "seq", split_axis=0, concat_axis=1, tiled=True))
 
     by_owner = full_second.reshape(BLOCK // outer_rows, outer_rows, BLOCK)
-    half = outer_rows // 2
+    half, quarter = outer_rows // 2, outer_rows // 4
     steps = [(q, 0, outer_rows) for q in range(CHUNKS - 1)]
-    steps += [(CHUNKS - 1, 0, half), (CHUNKS - 1, half, outer_rows - half)]
-    results, received = [], []
+    steps += [
+        (CHUNKS - 1, 0, half),
+        (CHUNKS - 1, half, quarter),
+        (CHUNKS - 1, half + quarter, outer_rows - half - quarter),
+    ]
+
+    def mix(n):
+        q, low, rows = steps[n]
+        factor = by_owner[:, low : low + rows].reshape(-1, BLOCK)
+        return lax.dot_general(
+            factor, sent[q], contract, preferred_element_type=jnp.float32
+        ).astype(jnp.bfloat16)
+
+    received = []
+    second = mix(0)
     for n, (q, low, rows) in enumerate(steps):
         ks = slice(q * k_sub, (q + 1) * k_sub)
-        factor = by_owner[:, low : low + rows].reshape(-1, BLOCK)
-        second = lax.dot_general(
-            factor, sent[q], contract, preferred_element_type=jnp.float32
-        ).astype(jnp.bfloat16)
-        if n >= 2:
-            second, received[n - 2] = lax.optimization_barrier((second, received[n - 2]))
-        returned = lax.all_to_all(second, "seq", split_axis=0, concat_axis=1, tiled=True)
+        after = None
+        if n + 1 < len(steps):
+            after = mix(n + 1)
+            second, after = lax.optimization_barrier((second, after))
+        ended = n - 2 if rows == outer_rows or low == 0 else n - 3
+        if ended >= 0:
+            second, received[ended] = lax.optimization_barrier((second, received[ended]))
+        returned = lax.all_to_all(
+            second.reshape(-1, rows, *second.shape[1:]), "seq", split_axis=0, concat_axis=0
+        )
+        second = after
+        if n >= 1:
+            returned, received[n - 1][0] = lax.optimization_barrier(
+                (returned, received[n - 1][0])
+            )
+        returned = jnp.transpose(returned, (1, 0, 2, 3)).reshape(rows, k_sub, channels)
         gated = (
             token_grid[low : low + rows, ks].astype(jnp.float32)
             * returned.astype(jnp.float32)
@@ -75,6 +97,8 @@
                 )
             parts.append(middle)
         received.append(parts)
+
+    result = jnp.zeros((outer_rows, BLOCK, channels), jnp.bfloat16)
     for n, (q, low, rows) in enumerate(steps):
         total = None
         for shift in range(n_ch):
@@ -82,9 +106,9 @@
                 received[n][shift], second_dense[shift], preferred_element_type=jnp.float32
             )
             total = term if total is None else total + term
-        results.append(total.astype(jnp.bfloat16).reshape(rows, k_sub, channels))
-    results[-2:] = [jnp.concatenate(results[-2:], axis=0)]
-    return jnp.concatenate(results, axis=1).reshape(tok_rows, channels)
+        part = total.astype(jnp.bfloat16).reshape(rows, k_sub, channels)
+        result = lax.dynamic_update_slice(result, part, (low, q * k_sub, 0))
+    return result.reshape(tok_rows, channels)
 
 
 def solution(mesh):

time: 1750 us -> 1690 us (0.966)
  waiting for transfers between devices: 1170 us -> 1110 us
  local copies, waits for them, and re-layouts: 153 us -> 190 us
  other arithmetic: 76.9 us -> 43.7 us
    ppermute x5 -> x6, waiting for transfers between devices: 178 us -> 30.6 us  [local(): lax.ppermute(middle, 'ch', [(d, (d + shift) % n_ch) for d in range(n_ch)])]
    all_to_all x5 -> x6, waiting for transfers between devices: 387 us -> 470 us  [local(): lax.all_to_all(second.reshape(-1, rows, *second.shape[1:]), 'seq', split_...]
    dynamic_update_slice x0 -> x6, local copies, waits for them, and re-layouts: none -> 35.9 us  [local(): result = lax.dynamic_update_slice(result, part, (low, q * k_sub, 0))]
    concatenate x1 -> x0, other arithmetic: 35.3 us -> none  [local(): return jnp.concatenate(results, axis=1).reshape(tok_rows, channels)]
    optimization_barrier x3 -> x6, local copies, waits for them, and re-layouts: 26.6 us -> 52.1 us  [the longest x4 26.5 us: local(): lax.optimization_barrier((second, received[ended]))]
    convert_element_type x2 -> x0, local copies, waits for them, and re-layouts: 25.1 us -> none  [local(): second = lax.dot_general(factor, sent[q], contract, preferred_element_typ...]
    dot_general x10 -> x12, matrix products: 103 us -> 89.3 us  [local(): jnp.dot(received[n][shift], second_dense[shift], preferred_element_type=j...]
    dot_general x8 -> x11, matrix products: 47.8 us -> 57.4 us  [local(): jnp.dot(gated, first_dense[shift], preferred_element_type=jnp.float32)]
  transfers between devices with their start and end apart: 14 -> 16, of which waited for: 12 -> 11; matrix products, arithmetic and copies ran while one was open for 23% -> 24% of each run, Pallas kernels for 0% -> 0%
where the time goes in v2:
time: 1690 us; the launch traced here: 1680 us
  waiting for transfers between devices  1110 us (66%)
  matrix products  261 us (15%)
  local copies, waits for them, and re-layouts  190 us (11%)
  starting transfers between devices  62.2 us (4%)
  other arithmetic  43.7 us (3%)
  blocking collectives  18.1 us (1%)
    all_to_all x4, waiting for transfers between devices, local(): lax.all_to_all(twisted, 'seq', split_axis=0, concat_axis=1, tiled=True)  607 us
    all_to_all x6, waiting for transfers between devices, local(): lax.all_to_all(second.reshape(-1, rows, *second.shape[1:]), 'seq', split_...  470 us
    dot_general x12, matrix products, local(): jnp.dot(received[n][shift], second_dense[shift], preferred_element_type=j...  89.3 us
    dot_general x4, matrix products, local(): lax.dot_general(full_first[ks], token_grid, contract, preferred_element_t...  65.8 us
    dot_general x11, matrix products, local(): jnp.dot(gated, first_dense[shift], preferred_element_type=jnp.float32)  57.4 us
    dot_general x6, matrix products, mix(): lax.dot_general(factor, sent[q], contract, preferred_element_type=jnp.flo...  48.8 us
    dynamic_update_slice x6, local copies, waits for them, and re-layouts, local(): result = lax.dynamic_update_slice(result, part, (low, q * k_sub, 0))  35.9 us
    convert_element_type x6, other arithmetic, local(): gated = (token_grid[low:low + rows, ks].astype(jnp.float32) * returned.as...  34.9 us
  transfers between devices with their start and end apart: 16, of which 11 were waited for; matrix products, arithmetic and copies ran while one was open for 24% of the time, Pallas kernels for 0%

profile of v2, /device:TPU:12, one launch (start us, length us, event | category | flops | bytes accessed | tf_op | source)
XLA Modules:
  0.0 1683.2 jit_solution(17699648303405418358)
XLA Ops:
  0.8 8.9 all_gather.6
  9.7 16.4 multiply_convert_fusion
  26.1 11.4 copy.96
  37.5 6.9 all-to-all-start.1
  44.4 16.4 multiply_convert_fusion.2
  60.8 11.4 copy.93
  72.2 154.2 %all-to-all-done.1 = bf16[128,32,1024]{2,1,0:T(8,128)(2,1)} async-done(((bf16[128,32,1024]{2,1,0:T(8,128)(2,1)}), bf16[128,32,1024]{2,1,0:T(8,128)(2,1)}, u32[]{:S(2)}, u32[]{:S(2)}) %all-to-all-start.1) | async-done | bytes 8388640 | tf_op jit(solution)/shard_map/all_to_all | solution.py:46
  231.5 9.2 all_gather.7
  240.7 16.6 multiply_convert_fusion.1
  257.3 16.4 multiply_convert_fusion.3
  273.7 8.5 copy.97
  282.2 131.5 %all-to-all-done = bf16[128,32,1024]{2,1,0:T(8,128)(2,1)} async-done(((bf16[128,32,1024]{2,1,0:T(8,128)(2,1)}), bf16[128,32,1024]{2,1,0:T(8,128)(2,1)}, u32[]{:S(2)}, u32[]{:S(2)}) %all-to-all-start) | async-done | bytes 8388640 | tf_op jit(solution)/shard_map/all_to_all | solution.py:46
  413.7 8.6 copy.94
  422.3 10.4 convert_bitcast_fusion.5
  432.7 6.9 convert_bitcast_fusion.6
  439.6 13.0 copy.106
  457.7 11.5 copy.99
  469.2 170.7 %all-to-all-done.5 = bf16[16,32,8,1024]{3,2,1,0:T(8,128)(2,1)} async-done(((bf16[16,32,8,1024]{3,2,1,0:T(8,128)(2,1)}), bf16[16,32,8,1024]{3,2,1,0:T(8,128)(2,1)}, u32[]{:S(2)}, u32[]{:S(2)}) %all-to-all-start.5) | async-done | bytes 8388640 | tf_op jit(solution)/shard_map/all_to_all | solution.py:75
  645.0 11.4 copy.102
  656.3 170.8 %all-to-all-done.2 = bf16[128,32,1024]{2,1,0:T(8,128)(2,1)} async-done(((bf16[128,32,1024]{2,1,0:T(8,128)(2,1)}), bf16[128,32,1024]{2,1,0:T(8,128)(2,1)}, u32[]{:S(2)}, u32[]{:S(2)}) %all-to-all-start.2) | async-done | bytes 8388640 | tf_op jit(solution)/shard_map/all_to_all | solution.py:46
  832.2 8.6 copy.100
  840.9 10.3 convert_bitcast_fusion.4
  851.1 12.6 copy.105
  863.7 150.7 %all-to-all-done.3 = bf16[128,32,1024]{2,1,0:T(8,128)(2,1)} async-done(((bf16[128,32,1024]{2,1,0:T(8,128)(2,1)}), bf16[128,32,1024]{2,1,0:T(8,128)(2,1)}, u32[]{:S(2)}, u32[]{:S(2)}) %all-to-all-start.3) | async-done | bytes 8388640 | tf_op jit(solution)/shard_map/all_to_all | solution.py:46
  1014.4 5.5 all-to-all-start.4
  1020.4 7.0 broadcast_multiply_fusion
  1027.4 5.9 mul.199
  1033.3 8.3 fusion.2
  1041.6 6.1 convolution_convert_fusion.4
  1049.2 5.9 mul.195
  1055.1 9.0 copy.103
  1064.1 8.0 convert_bitcast_fusion.9
  1072.1 6.1 convolution_convert_fusion.5
  1078.2 123.8 %all-to-all-done.4 = bf16[16,32,8,1024]{3,2,1,0:T(8,128)(2,1)} async-done(((bf16[16,32,8,1024]{3,2,1,0:T(8,128)(2,1)}), bf16[16,32,8,1024]{3,2,1,0:T(8,128)(2,1)}, u32[]{:S(2)}, u32[]{:S(2)}) %all-to-all-start.4) | async-done | bytes 8388640 | tf_op jit(solution)/shard_map/all_to_all | solution.py:75
  1202.0 12.6 copy.114
  1214.6 5.6 all-to-all-start.6
  1220.2 7.9 fusion.1
  1228.1 6.1 convolution_convert_fusion.2
  1243.6 7.3 convert_bitcast_fusion.11
  1250.9 5.9 convert_bitcast_fusion.10
  1256.8 6.3 convolution_convert_fusion.3
  1263.1 139.1 %all-to-all-done.6 = bf16[16,32,8,1024]{3,2,1,0:T(8,128)(2,1)} async-done(((bf16[16,32,8,1024]{3,2,1,0:T(8,128)(2,1)}), bf16[16,32,8,1024]{3,2,1,0:T(8,128)(2,1)}, u32[]{:S(2)}, u32[]{:S(2)}) %all-to-all-start.6) | async-done | bytes 8388640 | tf_op jit(solution)/shard_map/all_to_all | solution.py:75
  1402.2 6.8 copy.116
  1414.0 10.8 fusion.13
  1424.8 11.3 add_convert_fusion.2
  1436.2 13.5 dynamic_update_slice.18
  1453.8 8.0 fusion
  1461.8 6.1 convolution_convert_fusion
  1469.4 8.2 fusion.14
  1477.6 28.8 %all-to-all-done.7 = bf16[16,16,8,1024]{3,2,1,0:T(8,128)(2,1)} async-done(((bf16[16,16,8,1024]{3,2,1,0:T(8,128)(2,1)}), bf16[16,16,8,1024]{3,2,1,0:T(8,128)(2,1)}, u32[]{:S(2)}, u32[]{:S(2)}) %all-to-all-start.7) | async-done | bytes 4194336 | tf_op jit(solution)/shard_map/all_to_all | solution.py:75
  1506.4 5.4 all-to-all-start.8
  1511.8 11.4 add_convert_fusion.1
  1523.2 8.5 constant_dynamic-update-slice_fusion.4
  1531.7 9.5 convolution_convert_fusion.1
  1551.6 7.4 all-to-all-done.8
  1576.8 5.6 all-to-all-start.9
  1582.4 10.5 fusion.15
  1592.9 5.6 fusion.16
  1598.6 11.6 add_convert_fusion
  1610.1 8.4 constant_dynamic-update-slice_fusion.3
  1618.5 18.2 %collective-permute-done.3 = bf16[2048,512]{1,0:T(8,128)(2,1)} collective-permute-done((bf16[2048,512]{1,0:T(8,128)(2,1)}, bf16[2048,512]{1,0:T(8,128)(2,1)}, u32[]{:S(2)}, u32[]{:S(2)}) %collective-permute-start.3) | collective-permute-done | bytes 2097184 | tf_op jit(solution)/shard_map/ppermute | solution.py:95
  1636.7 6.4 add_convert_fusion.3
  1659.5 5.9 fusion.6
  1665.3 12.3 collective-permute-done.5
  (107 shorter events, 92.8 us)
Async XLA Ops:
  37.5 188.9 %all-to-all-start.1 = ((bf16[128,32,1024]{2,1,0:T(8,128)(2,1)}), bf16[128,32,1024]{2,1,0:T(8,128)(2,1)}, u32[]{:S(2)}, u32[]{:S(2)}) async-start(bf16[128,32,1024]{2,1,0:T(8,128)(2,1)} %copy.96), calls=%async_computation.1 | async-start | bytes 16777216 | tf_op jit(solution)/shard_map/all_to_all | solution.py:46
  72.2 159.2 %copy-start.21 = (bf16[256,512]{1,0:T(8,128)(2,1)S(1)}, bf16[256,512]{1,0:T(8,128)(2,1)}, u32[]{:S(2)}) copy-start(bf16[256,512]{1,0:T(8,128)(2,1)} %param.9) | copy-start | bytes 786436
  226.4 187.2 %all-to-all-start = ((bf16[128,32,1024]{2,1,0:T(8,128)(2,1)}), bf16[128,32,1024]{2,1,0:T(8,128)(2,1)}, u32[]{:S(2)}, u32[]{:S(2)}) async-start(bf16[128,32,1024]{2,1,0:T(8,128)(2,1)} %copy.93), calls=%async_computation | async-start | bytes 16777216 | tf_op jit(solution)/shard_map/all_to_all | solution.py:46
  240.7 808.5 %copy-start.6 = (bf16[512,512]{1,0:T(8,128)(2,1)}, bf16[512,512]{1,0:T(8,128)(2,1)S(1)}, u32[]{:S(2)}) copy-start(bf16[512,512]{1,0:T(8,128)(2,1)S(1)} %all_gather.7) | copy-start | bytes 1572868
  422.3 10.4 copy-start.3
  452.6 187.3 %all-to-all-start.5 = ((bf16[16,32,8,1024]{3,2,1,0:T(8,128)(2,1)}), bf16[16,32,8,1024]{3,2,1,0:T(8,128)(2,1)}, u32[]{:S(2)}, u32[]{:S(2)}) async-start(bf16[16,32,8,1024]{3,2,1,0:T(8,128)(2,1)} %bitcast.213), calls=%async_computation.5 | async-start | bytes 16777216 | tf_op jit(solution)/shard_map/all_to_all | solution.py:75
  639.9 187.3 %all-to-all-start.2 = ((bf16[128,32,1024]{2,1,0:T(8,128)(2,1)}), bf16[128,32,1024]{2,1,0:T(8,128)(2,1)}, u32[]{:S(2)}, u32[]{:S(2)}) async-start(bf16[128,32,1024]{2,1,0:T(8,128)(2,1)} %copy.99), calls=%async_computation.2 | async-start | bytes 16777216 | tf_op jit(solution)/shard_map/all_to_all | solution.py:46
  827.2 187.3 %all-to-all-start.3 = ((bf16[128,32,1024]{2,1,0:T(8,128)(2,1)}), bf16[128,32,1024]{2,1,0:T(8,128)(2,1)}, u32[]{:S(2)}, u32[]{:S(2)}) async-start(bf16[128,32,1024]{2,1,0:T(8,128)(2,1)} %copy.102), calls=%async_computation.3 | async-start | bytes 16777216 | tf_op jit(solution)/shard_map/all_to_all | solution.py:46
  1014.4 5.5 copy-start.22
  1014.4 187.6 %all-to-all-start.4 = ((bf16[16,32,8,1024]{3,2,1,0:T(8,128)(2,1)}), bf16[16,32,8,1024]{3,2,1,0:T(8,128)(2,1)}, u32[]{:S(2)}, u32[]{:S(2)}) async-start(bf16[16,32,8,1024]{3,2,1,0:T(8,128)(2,1)} %bitcast.211), calls=%async_computation.4 | async-start | bytes 16777216 | tf_op jit(solution)/shard_map/all_to_all | solution.py:75
  1033.3 194.8 %copy-start.13 = (bf16[1024,512]{1,0:T(8,128)(2,1)}, bf16[1024,512]{1,0:T(8,128)(2,1)S(1)}, u32[]{:S(2)}) copy-start(bf16[1024,512]{1,0:T(8,128)(2,1)S(1)} %mul.199) | copy-start | bytes 3145732
  1041.6 6.1 copy-start.2
  1047.7 154.3 %collective-permute-start = (bf16[4096,512]{1,0:T(8,128)(2,1)}, bf16[4096,512]{1,0:T(8,128)(2,1)}, u32[]{:S(2)}, u32[]{:S(2)}) collective-permute-start(bf16[4096,512]{1,0:T(8,128)(2,1)} %convolution_convert_fusion.4), channel_id=1, source_target_pairs={{0,1},{1,0},{2,3},{3,2},{4,5},{5,4},{6,7},{7,6},{8,9},{9,8},{10,11... | collective-permute-start | bytes 12582920 | tf_op jit(solution)/shard_map/ppermute | solution.py:95
  1055.1 17.0 %copy-start.9 = (bf16[1024,512]{1,0:T(8,128)(2,1)}, bf16[1024,512]{1,0:T(8,128)(2,1)S(1)}, u32[]{:S(2)}) copy-start(bf16[1024,512]{1,0:T(8,128)(2,1)S(1)} %mul.195) | copy-start | bytes 3145732
  1055.1 17.0 %slice-start.2 = ((s8[8388608]{0:T(1024)(128)(4,1)}), s8[4194304]{0:T(1024)(128)(4,1)S(1)}, s32[]{:S(2)}) async-start(s8[8388608]{0:T(1024)(128)(4,1)} %bitcast.222), calls=%async_computation.12 | async-start | bytes 8388608
  1064.1 8.0 slice-start.3
  1214.6 187.6 %all-to-all-start.6 = ((bf16[16,32,8,1024]{3,2,1,0:T(8,128)(2,1)}), bf16[16,32,8,1024]{3,2,1,0:T(8,128)(2,1)}, u32[]{:S(2)}, u32[]{:S(2)}) async-start(bf16[16,32,8,1024]{3,2,1,0:T(8,128)(2,1)} %bitcast.212), calls=%async_computation.6 | async-start | bytes 16777216 | tf_op jit(solution)/shard_map/all_to_all | solution.py:75
  1228.1 6.1 copy-start
  1228.1 7.6 copy-start.20
  1234.2 168.0 %collective-permute-start.1 = (bf16[4096,512]{1,0:T(8,128)(2,1)}, bf16[4096,512]{1,0:T(8,128)(2,1)}, u32[]{:S(2)}, u32[]{:S(2)}) collective-permute-start(bf16[4096,512]{1,0:T(8,128)(2,1)} %convolution_convert_fusion.2), channel_id=1, source_target_pairs={{0,1},{1,0},{2,3},{3,2},{4,5},{5,4},{6,7},{7,6},{8,9},{9,8},{10,11... | collective-permute-start | bytes 12582920 | tf_op jit(solution)/shard_map/ppermute | solution.py:95
  1243.6 13.2 slice-start
  1250.9 6.0 slice-start.1
  1250.9 6.0 copy-start.10
  1409.0 97.4 %all-to-all-start.7 = ((bf16[16,16,8,1024]{3,2,1,0:T(8,128)(2,1)}), bf16[16,16,8,1024]{3,2,1,0:T(8,128)(2,1)}, u32[]{:S(2)}, u32[]{:S(2)}) async-start(bf16[16,16,8,1024]{3,2,1,0:T(8,128)(2,1)} %bitcast.214), calls=%async_computation.7 | async-start | bytes 8388608 | tf_op jit(solution)/shard_map/all_to_all | solution.py:75
  1414.0 10.8 copy-start.16
  1453.8 8.0 copy-start.14
  1461.8 6.2 copy-start.1
  1461.8 7.6 copy-start.17
  1461.8 7.6 copy-start.25
  1468.0 105.8 %collective-permute-start.2 = (bf16[4096,512]{1,0:T(8,128)(2,1)}, bf16[4096,512]{1,0:T(8,128)(2,1)}, u32[]{:S(2)}, u32[]{:S(2)}) collective-permute-start(bf16[4096,512]{1,0:T(8,128)(2,1)} %convolution_convert_fusion), channel_id=1, source_target_pairs={{0,1},{1,0},{2,3},{3,2},{4,5},{5,4},{6,7},{7,6},{8,9},{9,8},{10,11... | collective-permute-start | bytes 12582920 | tf_op jit(solution)/shard_map/ppermute | solution.py:95
  1506.4 52.6 %all-to-all-start.8 = ((bf16[16,8,8,1024]{3,2,1,0:T(8,128)(2,1)}), bf16[16,8,8,1024]{3,2,1,0:T(8,128)(2,1)}, u32[]{:S(2)}, u32[]{:S(2)}) async-start(bf16[16,8,8,1024]{3,2,1,0:T(8,128)(2,1)} %bitcast.230), calls=%async_computation.8 | async-start | bytes 4194304 | tf_op jit(solution)/shard_map/all_to_all | solution.py:75
  1523.2 8.5 copy-start.11
  1545.9 2.0 copy-start.4
  1559.0 8.3 copy-start.5
  1559.0 8.3 copy-start.15
  1565.8 5.7 copy-start.12
  1565.8 89.4 %collective-permute-start.4 = (bf16[1024,512]{1,0:T(8,128)(2,1)}, bf16[1024,512]{1,0:T(8,128)(2,1)}, u32[]{:S(2)}, u32[]{:S(2)}) collective-permute-start(bf16[1024,512]{1,0:T(8,128)(2,1)} %convolution_convert_fusion.10), channel_id=1, source_target_pairs={{0,1},{1,0},{2,3},{3,2},{4,5},{5,4},{6,7},{7,6},{8,9},{9,8},{10,11... | collective-permute-start | bytes 3145736 | tf_op jit(solution)/shard_map/ppermute | solution.py:95
  1571.0 65.8 %collective-permute-start.3 = (bf16[2048,512]{1,0:T(8,128)(2,1)}, bf16[2048,512]{1,0:T(8,128)(2,1)}, u32[]{:S(2)}, u32[]{:S(2)}) collective-permute-start(bf16[2048,512]{1,0:T(8,128)(2,1)} %convolution_convert_fusion.6), channel_id=1, source_target_pairs={{0,1},{1,0},{2,3},{3,2},{4,5},{5,4},{6,7},{7,6},{8,9},{9,8},{10,11... | collective-permute-start | bytes 6291464 | tf_op jit(solution)/shard_map/ppermute | solution.py:95
  1576.8 68.8 %all-to-all-start.9 = ((bf16[16,8,8,1024]{3,2,1,0:T(8,128)(2,1)}), bf16[16,8,8,1024]{3,2,1,0:T(8,128)(2,1)S(1)}, u32[]{:S(2)}, u32[]{:S(2)}) async-start(bf16[16,8,8,1024]{3,2,1,0:T(8,128)(2,1)} %bitcast.231), calls=%async_computation.9 | async-start | bytes 4194304 | tf_op jit(solution)/shard_map/all_to_all | solution.py:75
  1582.4 10.5 copy-start.18
  1582.4 10.5 copy-start.24
  1645.6 8.4 copy-start.19
  1645.6 8.4 copy-start.23
  1648.3 4.2 copy-start.7
  1652.5 25.2 %collective-permute-start.5 = (bf16[1024,512]{1,0:T(8,128)(2,1)}, bf16[1024,512]{1,0:T(8,128)(2,1)}, u32[]{:S(2)}, u32[]{:S(2)}) collective-permute-start(bf16[1024,512]{1,0:T(8,128)(2,1)} %convolution_convert_fusion.8), channel_id=1, source_target_pairs={{0,1},{1,0},{2,3},{3,2},{4,5},{5,4},{6,7},{7,6},{8,9},{9,8},{10,11... | collective-permute-start | bytes 3145736 | tf_op jit(solution)/shard_map/ppermute | solution.py:95
  1655.2 4.2 copy-start.8
